TPU v7x, 512 devices: a whole 4x4x16 slice. The times are simulated.
512 devices in a mesh: seq: 64 (over x, z), head: 8 (over y, core).
Axes of the slice: x: 4, y: 4, z: 16, core: 2. Of those that a mesh axis runs over, the one named last changes fastest.
Arguments:
- tokens: bfloat16 [16384, 5376], P('seq', 'head'), may hold values from -6 to 6
- features: bfloat16 [512, 64, 1152], P('seq'), may hold values from -6 to 6
- starts: int32 [8], replicated, may hold values from 0 to 16128, as said below
- sources: int32 [8], replicated, may hold values from 0 to 56, as said below
- soft_gain: float32 [1152], replicated, may hold values from 0.25 to 1.75
- proj_weight: bfloat16 [1152, 5376], P(None, 'head'), may hold values from -0.1875 to 0.1875
- input_gain: float32 [5376], replicated, may hold values from 0.25 to 1.75
- query_weight: bfloat16 [5376, 2048], P('seq', 'head'), may hold values from -0.078125 to 0.078125
- key_weight: bfloat16 [5376, 1024], P('seq', 'head'), may hold values from -0.078125 to 0.078125
- value_weight: bfloat16 [5376, 1024], P('seq', 'head'), may hold values from -0.078125 to 0.078125
- query_gain: float32 [128], replicated, may hold values from 0.25 to 1.75
- key_gain: float32 [128], replicated, may hold values from 0.25 to 1.75
- out_weight: bfloat16 [2048, 5376], P('seq', 'head'), may hold values from -0.125 to 0.125
- post_gain: float32 [5376], P('head'), may hold values from 0.25 to 1.75
Outputs:
- layer_out: bfloat16 [16384, 5376], P('seq', 'head')
Inputs may be any that keep to these rules, and one draw needn't show every extreme that they name: Image i takes positions starts[i] to starts[i] + 255; the spans are in increasing order of i, do not intersect, and each crosses one boundary between sequence shards. Distinct multiples of 8; image i's patches fill feature rows sources[i] * 8 onward.
All inputs are finite; a program needn't handle non-finite values.
Results may differ from a plain program's by a relative error of at most 0.012.
Values may be sent and summed in bfloat16 or wider, within the bound.
No kernel may reach another device: no remote copies, remote signals or barrier semaphores. Data moves between devices by JAX's collectives and lax.ppermute only.
A program may use at most 64 MiB of HBM per device.

v0:
```python
import jax
import jax.numpy as jnp
from jax import lax
from jax.sharding import PartitionSpec as P

D = 5376
HEAD_DIM = 128
WINDOW = 1024
PATCH_SIDE = 64
POOL = 4
IMG_TOK = 256
EPSILON = 1e-06
QUERY_SCALE = 168.0 ** (-0.5)
ROPE_BASE = 10000.0


def shifted(value, axis, steps):
    count = lax.axis_size(axis)
    leading, last = (max(0, -steps), min(count, count - steps))
    return lax.ppermute(value, axis, [(source, source + steps) for source in range(leading, last)])


def rms_scale(inputs, scale_gain):
    return (
        inputs * lax.rsqrt(jnp.mean(inputs * inputs, axis=-1, keepdims=True) + EPSILON) * scale_gain
    )


def rotate(inputs, positions):
    half_dim = inputs.shape[-1] // 2
    frequency = ROPE_BASE ** (-jnp.arange(half_dim, dtype=jnp.float32) * 2.0 / inputs.shape[-1])
    angles = positions.astype(jnp.float32)[:, None] * frequency[None, :]
    cosine = jnp.cos(angles)[:, None, :]
    sine_part = jnp.sin(angles)[:, None, :]
    first_half = inputs[..., :half_dim]
    second = inputs[..., half_dim:]
    return jnp.concatenate(
        [first_half * cosine - second * sine_part, second * cosine + first_half * sine_part],
        axis=-1,
    )


def image_of(positions, starts):
    inside = (positions[:, None] >= starts[None, :]) & (
        positions[:, None] < starts[None, :] + IMG_TOK
    )
    labels = jnp.arange(1, starts.shape[0] + 1, dtype=jnp.int32)
    return jnp.sum(jnp.where(inside, labels[None, :], 0), axis=1) - 1


def allowed_keys(query_pos, key_pos, starts, total_rows):
    query_img = image_of(query_pos, starts)
    key_img = image_of(key_pos, starts)
    inside = (key_pos >= 0) & (key_pos < total_rows)
    in_window = query_pos[:, None] - key_pos[None, :] < WINDOW
    causal = key_pos[None, :] <= query_pos[:, None]
    same_image = (query_img[:, None] == key_img[None, :]) & (query_img[:, None] >= 0)
    return inside[None, :] & in_window & (causal | same_image)


def attend(queries, key_rows, values, allowed):
    scores = jnp.einsum("qgrd,kgd->grqk", queries, key_rows, preferred_element_type=jnp.float32)
    scores = jnp.where(allowed[None, None], scores, -jnp.inf)
    row_max = jnp.max(scores, axis=-1, keepdims=True)
    weights = jnp.exp(scores - row_max)
    row_sum = jnp.sum(weights, axis=-1)
    mixed_heads = jnp.einsum(
        "grqk,kgd->qgrd", weights.astype(jnp.bfloat16), values, preferred_element_type=jnp.float32
    )
    return (mixed_heads / jnp.transpose(row_sum, (2, 0, 1))[..., None]).astype(jnp.bfloat16)


def body(
    tokens,
    features,
    starts,
    sources,
    soft_gain,
    proj_weight,
    input_gain,
    query_weight,
    key_weight,
    value_weight,
    query_gain,
    key_gain,
    out_weight,
    post_gain,
):
    tok_rows = tokens.shape[0]
    seq_count = lax.axis_size("seq")
    seq_index = lax.axis_index("seq")
    total_rows = seq_count * tok_rows
    image_count = starts.shape[0]
    my_pos = seq_index * tok_rows + jnp.arange(tok_rows, dtype=jnp.int32)
    pooled_side = PATCH_SIDE // POOL
    pool_rows = features.shape[0] // POOL
    block_rows = pool_rows * pooled_side
    shards_each = pooled_side // pool_rows
    patch_grid = features.reshape(pool_rows, POOL, pooled_side, POOL, features.shape[2])
    pooled = jnp.sum(patch_grid, axis=(1, 3), dtype=jnp.float32).reshape(
        block_rows, features.shape[2]
    ) / (POOL * POOL)
    soft = rms_scale(pooled, soft_gain).astype(jnp.bfloat16)
    embedded = jnp.dot(soft, proj_weight, preferred_element_type=jnp.float32).astype(jnp.bfloat16)
    gathered = lax.all_gather(embedded, "seq", axis=0, tiled=True)
    my_image = image_of(my_pos, starts)
    image_ids = jnp.arange(image_count, dtype=jnp.int32)
    row_base = sources // shards_each * (block_rows * shards_each) - starts
    offset_rows = jnp.sum(
        jnp.where(my_image[:, None] == image_ids[None, :], row_base[None, :], 0), axis=1
    )
    row_index = jnp.where(my_image >= 0, offset_rows + my_pos, 0)
    picked = jnp.take(gathered, row_index, axis=0)
    residual = jnp.where((my_image >= 0)[:, None], picked, tokens)
    whole_rows = lax.all_gather(residual, "head", axis=1, tiled=True)
    normed = rms_scale(whole_rows.astype(jnp.float32), input_gain).astype(jnp.bfloat16)

    def add_rows(piece_rows):
        return jnp.dot(normed, piece_rows, preferred_element_type=jnp.float32)

    query_sum = add_rows(lax.all_gather(query_weight, "seq", axis=0, tiled=True))
    key_sum = add_rows(lax.all_gather(key_weight, "seq", axis=0, tiled=True))
    value_sum = add_rows(lax.all_gather(value_weight, "seq", axis=0, tiled=True))
    kv_local = key_weight.shape[1] // HEAD_DIM
    group_size = query_weight.shape[1] // key_weight.shape[1]
    queries = (
        rotate(
            rms_scale(query_sum.reshape(tok_rows, kv_local * group_size, HEAD_DIM), query_gain),
            my_pos,
        )
        * QUERY_SCALE
    )
    queries = queries.astype(jnp.bfloat16).reshape(tok_rows, kv_local, group_size, HEAD_DIM)
    own_keys = (
        rotate(rms_scale(key_sum.reshape(tok_rows, kv_local, HEAD_DIM), key_gain), my_pos)
        .astype(jnp.bfloat16)
        .reshape(tok_rows, kv_local * HEAD_DIM)
    )
    own_values = value_sum.astype(jnp.bfloat16)
    past_count = WINDOW // tok_rows
    key_value = (own_keys, own_values)
    earlier = [
        shifted((key_value[0], key_value[1]), "seq", step_back)
        for step_back in range(past_count, 0, -1)
    ]
    past_keys = jnp.concatenate([entry[0] for entry in earlier], axis=0)
    past_values = jnp.concatenate([entry[1] for entry in earlier], axis=0)
    later = [shifted((key_value[0], key_value[1]), "seq", -1)]
    all_keys = jnp.concatenate([past_keys, own_keys] + [entry[0] for entry in later], axis=0)
    all_values = jnp.concatenate([past_values, own_values] + [entry[1] for entry in later], axis=0)
    key_pos = (seq_index - past_count) * tok_rows + jnp.arange(all_keys.shape[0], dtype=jnp.int32)
    allowed = allowed_keys(my_pos, key_pos, starts, total_rows)
    attended = attend(
        queries,
        all_keys.reshape(-1, kv_local, HEAD_DIM),
        all_values.reshape(-1, kv_local, HEAD_DIM),
        allowed,
    )
    attended = attended.reshape(tok_rows, kv_local * group_size * HEAD_DIM)
    heads_all = lax.all_gather(attended, "head", axis=1, tiled=True)
    projected = jnp.dot(
        heads_all,
        lax.all_gather(out_weight, "seq", axis=0, tiled=True),
        preferred_element_type=jnp.float32,
    )
    squares = lax.psum(jnp.sum(projected * projected, axis=1), "head")
    post = projected * lax.rsqrt(squares[:, None] / D + EPSILON) * post_gain
    return (residual.astype(jnp.float32) + post).astype(jnp.bfloat16)


def solution(mesh):
    return jax.shard_map(
        body,
        mesh=mesh,
        in_specs=(
            P("seq", "head"),
            P("seq", None, None),
            P(),
            P(),
            P(),
            P(None, "head"),
            P(),
            P("seq", "head"),
            P("seq", "head"),
            P("seq", "head"),
            P(),
            P(),
            P("seq", "head"),
            P("head"),
        ),
        out_specs=P("seq", "head"),
        check_vma=False,
    )
```

profile of v0, /device:TPU:1, one launch (start us, length us, event | category | flops | bytes accessed | tf_op | source)
XLA Modules:
  0.0 813.5 jit_solution(580391868668039390)
XLA Ops:
  6.5 3.4 reshape.416
  9.9 2.3 reduce_sum.100
  12.5 1.2 convolution_convert_fusion.1
  13.8 0.7 all-gather.21.cloned.1.call-update
  14.5 0.7 all-gather.19.cloned.1.call-update
  16.1 138.9 %all-gather.11.cloned.1.call-done = bf16[2048,672]{1,0:T(8,128)(2,1)} async-done(((bf16[32,672]{1,0:T(8,128)(2,1)}), bf16[2048,672]{1,0:T(8,128)(2,1)}) %all-gather.11.cloned.1.call-update) | async-done | bytes 2752528 | tf_op jit(solution)/shard_map/all_gather | solution.py:105
  155.0 3.7 gather_fusion
  158.9 0.8 select_select_fusion
  160.4 1.2 multiply_cosine_fusion
  161.7 1.4 fusion.11
  163.1 128.6 %all-gather.21.cloned.1.call-done = bf16[64,84,128]{2,1,0:T(8,128)(2,1)} async-done(((bf16[1,84,128]{2,1,0:T(8,128)(2,1)}), bf16[64,84,128]{2,1,0:T(8,128)(2,1)}) %all-gather.21.cloned.1.call-update) | async-done | bytes 1376272 | tf_op jit(solution)/shard_map/all_gather | solution.py:122
  291.6 3.2 reshape.428
  294.9 135.7 %all-gather.19.cloned.1.call-done = bf16[64,84,128]{2,1,0:T(8,128)(2,1)} async-done(((bf16[1,84,128]{2,1,0:T(8,128)(2,1)}), bf16[64,84,128]{2,1,0:T(8,128)(2,1)}) %all-gather.19.cloned.1.call-update) | async-done | bytes 1376272 | tf_op jit(solution)/shard_map/all_gather | solution.py:123
  430.6 2.2 reshape.426
  432.8 140.1 %all-gather.23.cloned.1.call-done = bf16[64,84,256]{2,1,0:T(8,128)(2,1)} async-done(((bf16[1,84,256]{2,1,0:T(8,128)(2,1)}), bf16[64,84,256]{2,1,0:T(8,128)(2,1)}) %all-gather.23.cloned.1.call-update) | async-done | bytes 2752528 | tf_op jit(solution)/shard_map/all_gather | solution.py:121
  572.9 5.1 reshape.430
  578.0 34.9 %all-gather.13.cloned.1.call-done = bf16[256,5376]{0,1:T(8,128)(2,1)} async-done(((bf16[256,672]{0,1:T(8,128)(2,1)}), bf16[256,5376]{0,1:T(8,128)(2,1)}) %all-gather.13.cloned.1.call-update) | async-done | bytes 2752528 | tf_op jit(solution)/shard_map/all_gather | solution.py:115
  612.9 2.7 fusion
  615.6 3.0 multiply_reduce_fusion.3
  619.0 0.6 pad_maximum_fusion
  619.7 8.1 collective-permute-start.5
  627.8 5.8 collective-permute-start.6
  633.5 4.5 collective-permute-start.7
  638.0 2.3 collective-permute-start.8
  640.3 1.3 collective-permute-start.9
  641.6 2.5 multiply_reduce_fusion.1
  644.1 1.8 copy.31
  645.9 1.1 multiply_multiply_fusion
  647.0 3.6 convolution_convert_fusion
  650.8 4.2 collective-permute-start
  655.0 0.8 constant_dynamic-update-slice_fusion.11
  655.9 1.3 collective-permute-start.1
  657.2 0.8 constant_dynamic-update-slice_fusion.10
  658.0 3.7 collective-permute-start.2
  661.8 0.8 constant_dynamic-update-slice_fusion.9
  662.6 4.2 collective-permute-start.3
  666.8 0.8 constant_dynamic-update-slice_fusion.8
  667.7 1.3 collective-permute-start.4
  669.1 1.8 collective-permute-done.3
  670.9 0.8 constant_dynamic-update-slice_fusion.6
  671.8 1.4 collective-permute-done.4
  673.1 0.7 fusion.46
  674.3 1.3 fusion.18
  675.7 78.1 %all-gather.17.cloned.1.call-done = bf16[2048,672]{1,0:T(8,128)(2,1)} async-done(((bf16[32,672]{1,0:T(8,128)(2,1)}), bf16[2048,672]{1,0:T(8,128)(2,1)}) %all-gather.17.cloned.1.call-update) | async-done | bytes 2752528 | tf_op jit(solution)/shard_map/all_gather | solution.py:163
  753.8 36.4 %all-gather.15.cloned.1.call-done = bf16[256,2048]{0,1:T(8,128)(2,1)} async-done(((bf16[256,256]{0,1:T(8,128)(2,1)}), bf16[256,2048]{0,1:T(8,128)(2,1)}) %all-gather.15.cloned.1.call-update) | async-done | bytes 1048592 | tf_op jit(solution)/shard_map/all_gather | solution.py:160
  790.2 3.5 multiply_reduce_fusion
  793.7 12.0 %psum.7 = f32[256]{0:T(256)S(1)} all-reduce(f32[256]{0:T(256)S(1)} %get-tuple-element.21), channel_id=1, replica_groups=mesh['seq'=64,'head'=8] {'head'}, use_global_device_ids=true, to_apply=%region_11.12 | all-reduce | flops 256 | bytes 2048 | tf_op jit(solution)/shard_map/psum | solution.py:166
  805.7 0.9 add_convert_fusion
  (79 shorter events, 3.3 us)
Async XLA Ops:
  6.5 6.0 copy-start
  6.5 5.8 copy-start.6
  6.5 148.5 %all-gather.11.cloned.1.call-start = ((), (), s32[]{:S(2)}) async-start(), calls=%async_computation | async-start | bytes 3194880 | tf_op jit(solution)/shard_map/all_gather | solution.py:105
  9.9 5.9 copy-start.7
  9.9 5.9 copy-start.11
  12.5 146.4 %copy-start.5 = (bf16[256,672]{0,1:T(8,128)(2,1)S(1)}, bf16[256,672]{0,1:T(8,128)(2,1)}, u32[]{:S(2)}) copy-start(bf16[256,672]{0,1:T(8,128)(2,1)} %param.14) | copy-start | bytes 1032196
  13.7 277.9 %all-gather.21.cloned.1.call-start = ((), (), s32[]{:S(2)}) async-start(), calls=%async_computation.5 | async-start | bytes 1464320 | tf_op jit(solution)/shard_map/all_gather | solution.py:122
  14.5 416.1 %all-gather.19.cloned.1.call-start = ((), (), s32[]{:S(2)}) async-start(), calls=%async_computation.4 | async-start | bytes 1464320 | tf_op jit(solution)/shard_map/all_gather | solution.py:123
  15.2 557.7 %all-gather.23.cloned.1.call-start = ((), (), s32[]{:S(2)}) async-start(), calls=%async_computation.6 | async-start | bytes 2928640 | tf_op jit(solution)/shard_map/all_gather | solution.py:121
  15.8 597.1 %all-gather.13.cloned.1.call-start = ((), (), s32[]{:S(2)}) async-start(), calls=%async_computation.1 | async-start | bytes 3096576 | tf_op jit(solution)/shard_map/all_gather | solution.py:115
  159.7 594.1 %all-gather.17.cloned.1.call-start = ((), (), s32[]{:S(2)}) async-start(), calls=%async_computation.3 | async-start | bytes 3194880 | tf_op jit(solution)/shard_map/all_gather | solution.py:163
  160.2 629.9 %all-gather.15.cloned.1.call-start = ((), (), s32[]{:S(2)}) async-start(), calls=%async_computation.2 | async-start | bytes 1179648 | tf_op jit(solution)/shard_map/all_gather | solution.py:160
  572.9 42.7 %copy-start.12 = (f32[5376]{0:T(1024)S(1)}, f32[5376]{0:T(1024)}, u32[]{:S(2)}) copy-start(f32[5376]{0:T(1024)} %param.20) | copy-start | bytes 64516
  612.9 2.7 copy-start.2
  615.6 3.0 copy-start.9
  615.6 26.0 %copy-start.3 = (bf16[5376,256]{1,0:T(8,128)(2,1)S(1)}, bf16[5376,256]{1,0:T(8,128)(2,1)}, u32[]{:S(2)}) copy-start(bf16[5376,256]{1,0:T(8,128)(2,1)} %reshape.430) | copy-start | bytes 8257540
  619.6 26.2 %copy-start.10 = (f32[128]{0:T(128)S(1)}, f32[128]{0:T(128)}, u32[]{:S(2)}) copy-start(f32[128]{0:T(128)} %param.24) | copy-start | bytes 1540
  619.7 31.1 %collective-permute-start.5 = (bf16[256,128]{0,1:T(8,128)(2,1)}, bf16[256,128]{0,1:T(8,128)(2,1)}, u32[]{:S(2)}, u32[]{:S(2)}) collective-permute-start(bf16[256,128]{0,1:T(8,128)(2,1)} %pad_maximum_fusion), channel_id=1, source_target_pairs={{0,32},{8,40},{16,48},{24,56},{32,64},{40,72},{48,80},{56,88},{64,... | collective-permute-start | bytes 196616 | tf_op jit(solution)/shard_map/ppermute | solution.py:20
  627.8 28.1 %collective-permute-start.6 = (bf16[256,128]{0,1:T(8,128)(2,1)}, bf16[256,128]{0,1:T(8,128)(2,1)}, u32[]{:S(2)}, u32[]{:S(2)}) collective-permute-start(bf16[256,128]{0,1:T(8,128)(2,1)} %pad_maximum_fusion), channel_id=1, source_target_pairs={{0,24},{8,32},{16,40},{24,48},{32,56},{40,64},{48,72},{56,80},{64,... | collective-permute-start | bytes 196616 | tf_op jit(solution)/shard_map/ppermute | solution.py:20
  633.5 24.5 %collective-permute-start.7 = (bf16[256,128]{0,1:T(8,128)(2,1)}, bf16[256,128]{0,1:T(8,128)(2,1)}, u32[]{:S(2)}, u32[]{:S(2)}) collective-permute-start(bf16[256,128]{0,1:T(8,128)(2,1)} %pad_maximum_fusion), channel_id=1, source_target_pairs={{0,16},{8,24},{16,32},{24,40},{32,48},{40,56},{48,64},{56,72},{64,... | collective-permute-start | bytes 196616 | tf_op jit(solution)/shard_map/ppermute | solution.py:20
  638.0 24.6 %collective-permute-start.8 = (bf16[256,128]{0,1:T(8,128)(2,1)}, bf16[256,128]{0,1:T(8,128)(2,1)}, u32[]{:S(2)}, u32[]{:S(2)}) collective-permute-start(bf16[256,128]{0,1:T(8,128)(2,1)} %pad_maximum_fusion), channel_id=1, source_target_pairs={{0,8},{8,16},{16,24},{24,32},{32,40},{40,48},{48,56},{56,64},{64,7... | collective-permute-start | bytes 196616 | tf_op jit(solution)/shard_map/ppermute | solution.py:20
  640.3 30.6 %collective-permute-start.9 = (bf16[256,128]{0,1:T(8,128)(2,1)}, bf16[256,128]{0,1:T(8,128)(2,1)}, u32[]{:S(2)}, u32[]{:S(2)}) collective-permute-start(bf16[256,128]{0,1:T(8,128)(2,1)} %pad_maximum_fusion), channel_id=1, source_target_pairs={{8,0},{16,8},{24,16},{32,24},{40,32},{48,40},{56,48},{64,56},{72,6... | collective-permute-start | bytes 196616 | tf_op jit(solution)/shard_map/ppermute | solution.py:20
  647.0 3.6 copy-start.4
  650.8 16.9 %collective-permute-start = (bf16[256,128]{1,0:T(8,128)(2,1)S(1)}, bf16[256,128]{1,0:T(8,128)(2,1)S(1)}, u32[]{:S(2)}, u32[]{:S(2)}) collective-permute-start(bf16[256,128]{1,0:T(8,128)(2,1)S(1)} %convolution_convert_fusion), channel_id=1, source_target_pairs={{0,32},{8,40},{16,48},{24,56},{32,64},{40,72},{48,80},{56,88},{64,... | collective-permute-start | bytes 196616 | tf_op jit(solution)/shard_map/ppermute | solution.py:20
  655.9 13.1 %collective-permute-start.1 = (bf16[256,128]{1,0:T(8,128)(2,1)S(1)}, bf16[256,128]{1,0:T(8,128)(2,1)S(1)}, u32[]{:S(2)}, u32[]{:S(2)}) collective-permute-start(bf16[256,128]{1,0:T(8,128)(2,1)S(1)} %convolution_convert_fusion), channel_id=1, source_target_pairs={{0,24},{8,32},{16,40},{24,48},{32,56},{40,64},{48,72},{56,80},{64,... | collective-permute-start | bytes 196616 | tf_op jit(solution)/shard_map/ppermute | solution.py:20
  658.0 11.0 %collective-permute-start.2 = (bf16[256,128]{1,0:T(8,128)(2,1)S(1)}, bf16[256,128]{1,0:T(8,128)(2,1)S(1)}, u32[]{:S(2)}, u32[]{:S(2)}) collective-permute-start(bf16[256,128]{1,0:T(8,128)(2,1)S(1)} %convolution_convert_fusion), channel_id=1, source_target_pairs={{0,16},{8,24},{16,32},{24,40},{32,48},{40,56},{48,64},{56,72},{64,... | collective-permute-start | bytes 196616 | tf_op jit(solution)/shard_map/ppermute | solution.py:20
  662.6 8.3 %collective-permute-start.3 = (bf16[256,128]{1,0:T(8,128)(2,1)S(1)}, bf16[256,128]{1,0:T(8,128)(2,1)S(1)}, u32[]{:S(2)}, u32[]{:S(2)}) collective-permute-start(bf16[256,128]{1,0:T(8,128)(2,1)S(1)} %convolution_convert_fusion), channel_id=1, source_target_pairs={{0,8},{8,16},{16,24},{24,32},{32,40},{40,48},{48,56},{56,64},{64,7... | collective-permute-start | bytes 196616 | tf_op jit(solution)/shard_map/ppermute | solution.py:20
  667.7 5.4 collective-permute-start.4
  675.6 130.1 %copy-start.1 = (bf16[256,672]{0,1:T(8,128)(2,1)S(1)}, bf16[256,672]{0,1:T(8,128)(2,1)}, u32[]{:S(2)}) copy-start(bf16[256,672]{0,1:T(8,128)(2,1)} %select_select_fusion) | copy-start | bytes 1032196
  675.6 130.1 %copy-start.8 = (f32[672]{0:T(1024)S(1)}, f32[672]{0:T(1024)}, u32[]{:S(2)}) copy-start(f32[672]{0:T(1024)} %param.27) | copy-start | bytes 8068
Sparse Core Ops, SparseCore 0:
  13.8 141.1 all-gather.10
  157.9 133.6 all-gather.20
  294.6 135.9 all-gather.18
  433.4 139.4 all-gather.22
  574.8 38.0 all-gather.12
  615.7 138.0 all-gather.16
  755.9 34.2 all-gather.14
where the time goes:
time: 815 us; the launch traced here: 814 us
  waiting for transfers between devices  698 us (86%)
  starting transfers between devices  37 us (5%)
  local copies, waits for them, and re-layouts  24.1 us (3%)
  matrix products  15.8 us (2%)
  between operations  13.9 us (2%)
  other arithmetic  12.5 us (2%)
  blocking collectives  12 us (1%)
    all_gather x1, waiting for transfers between devices, body(): lax.all_gather(query_weight, 'seq', axis=0, tiled=True)  140 us
    all_gather x1, waiting for transfers between devices, body(): gathered = lax.all_gather(embedded, 'seq', axis=0, tiled=True)  139 us
    all_gather x1, waiting for transfers between devices, body(): lax.all_gather(value_weight, 'seq', axis=0, tiled=True)  136 us
    all_gather x1, waiting for transfers between devices, body(): key_sum = add_rows(lax.all_gather(key_weight, 'seq', axis=0, tiled=True))  129 us
    all_gather x1, waiting for transfers between devices, body(): lax.all_gather(out_weight, 'seq', axis=0, tiled=True)  78.1 us
    ppermute x10, starting transfers between devices, shifted(): lax.ppermute(value, axis, [(source, source + steps) for source in range(l...  36.7 us
    all_gather x1, waiting for transfers between devices, body(): heads_all = lax.all_gather(attended, 'head', axis=1, tiled=True)  36.4 us
    all_gather x1, waiting for transfers between devices, body(): whole_rows = lax.all_gather(residual, 'head', axis=1, tiled=True)  34.9 us
  transfers between devices with their start and end apart: 17, of which 9 were waited for; matrix products, arithmetic and copies ran while one was open for 5% of the time, Pallas kernels for 0%

commit v1 on v0

--- a/solution.py
+++ b/solution.py
@@ -112,7 +112,12 @@
     row_index = jnp.where(my_image >= 0, offset_rows + my_pos, 0)
     picked = jnp.take(gathered, row_index, axis=0)
     residual = jnp.where((my_image >= 0)[:, None], picked, tokens)
-    whole_rows = lax.all_gather(residual, "head", axis=1, tiled=True)
+    ring = [residual]
+    for hop in range(7):
+        ring.append(lax.ppermute(ring[-1], "head", [(dev, (dev + 1) % 8) for dev in range(8)]))
+    whole_rows = jnp.roll(
+        jnp.concatenate(ring[::-1], axis=1), (lax.axis_index("head") + 1) * ring[0].shape[1], axis=1
+    )
     normed = rms_scale(whole_rows.astype(jnp.float32), input_gain).astype(jnp.bfloat16)
 
     def add_rows(piece_rows):

time: 815 us -> 776 us (0.952)
  waiting for transfers between devices: 698 us -> 643 us
  starting transfers between devices: 37 us -> 55.8 us
    all_gather x1, waiting for transfers between devices: 129 us -> 81.4 us  [body(): key_sum = add_rows(lax.all_gather(key_weight, 'seq', axis=0, tiled=True))]
    all_gather x1 -> x0, waiting for transfers between devices: 34.9 us -> none  [body(): whole_rows = lax.all_gather(residual, 'head', axis=1, tiled=True)]
    ppermute x0 -> x7, waiting for transfers between devices: none -> 26.3 us  [body(): lax.ppermute(ring[-1], 'head', [(dev, (dev + 1) % 8) for dev in range(8)])]
    ppermute x0 -> x7, starting transfers between devices: none -> 22.1 us  [body(): lax.ppermute(ring[-1], 'head', [(dev, (dev + 1) % 8) for dev in range(8)])]
    unnamed x38 -> x61, local copies, waits for them, and re-layouts: 14.1 us -> 19.8 us
  transfers between devices with their start and end apart: 17 -> 23, of which waited for: 9 -> 14; matrix products, arithmetic and copies ran while one was open for 5% -> 5% of each run, Pallas kernels for 0% -> 0%
where the time goes in v1:
time: 776 us; the launch traced here: 775 us
  waiting for transfers between devices  643 us (83%)
  starting transfers between devices  55.8 us (7%)
  local copies, waits for them, and re-layouts  27.3 us (4%)
  matrix products  14.4 us (2%)
  between operations  14.1 us (2%)
  blocking collectives  12 us (2%)
  other arithmetic  8.47 us (1%)
    all_gather x1, waiting for transfers between devices, body(): lax.all_gather(query_weight, 'seq', axis=0, tiled=True)  139 us
    all_gather x1, waiting for transfers between devices, body(): gathered = lax.all_gather(embedded, 'seq', axis=0, tiled=True)  139 us
    all_gather x1, waiting for transfers between devices, body(): lax.all_gather(value_weight, 'seq', axis=0, tiled=True)  136 us
    all_gather x1, waiting for transfers between devices, body(): key_sum = add_rows(lax.all_gather(key_weight, 'seq', axis=0, tiled=True))  81.4 us
    all_gather x1, waiting for transfers between devices, body(): lax.all_gather(out_weight, 'seq', axis=0, tiled=True)  80.1 us
    all_gather x1, waiting for transfers between devices, body(): heads_all = lax.all_gather(attended, 'head', axis=1, tiled=True)  36.3 us
    ppermute x10, starting transfers between devices, shifted(): lax.ppermute(value, axis, [(source, source + steps) for source in range(l...  33.4 us
    ppermute x7, waiting for transfers between devices, body(): lax.ppermute(ring[-1], 'head', [(dev, (dev + 1) % 8) for dev in range(8)])  26.3 us
  transfers between devices with their start and end apart: 23, of which 14 were waited for; matrix products, arithmetic and copies ran while one was open for 5% of the time, Pallas kernels for 0%

profile of v1, /device:TPU:1, one launch (start us, length us, event | category | flops | bytes accessed | tf_op | source)
XLA Modules:
  0.0 775.5 jit_solution(16858944279664613963)
XLA Ops:
  6.6 3.4 reshape.416
  10.0 2.2 reduce_sum.100
  12.5 1.2 convolution_convert_fusion.1
  16.1 138.9 %all-gather.10.cloned.1.call-done = bf16[2048,672]{1,0:T(8,128)(2,1)} async-done(((bf16[32,672]{1,0:T(8,128)(2,1)}), bf16[2048,672]{1,0:T(8,128)(2,1)}) %all-gather.10.cloned.1.call-update) | async-done | bytes 2752528 | tf_op jit(solution)/shard_map/all_gather | solution.py:105
  155.0 3.7 gather_fusion
  158.9 9.9 %collective-permute-start = (bf16[256,672]{0,1:T(8,128)(2,1)S(1)}, bf16[256,672]{0,1:T(8,128)(2,1)S(1)}, u32[]{:S(2)}, u32[]{:S(2)}) collective-permute-start(bf16[256,672]{0,1:T(8,128)(2,1)S(1)} %select_select_fusion), channel_id=1, source_target_pairs={{0,1},{1,2},{2,3},{3,4},{4,5},{5,6},{6,7},{7,0},{8,9},{9,10},{10,1... | collective-permute-start | bytes 1032200 | tf_op jit(solution)/shard_map/ppermute | solution.py:117
  168.8 4.2 collective-permute-done
  173.0 2.5 collective-permute-start.1
  175.5 4.2 collective-permute-done.1
  179.7 2.5 collective-permute-start.2
  182.2 4.2 collective-permute-done.2
  186.4 2.5 collective-permute-start.3
  189.0 4.1 collective-permute-done.3
  193.1 2.5 collective-permute-start.4
  195.7 4.8 collective-permute-done.4
  200.5 1.8 collective-permute-start.5
  202.2 1.4 fusion.11
  203.6 4.8 collective-permute-done.5
  209.0 1.2 multiply_cosine_fusion
  210.2 81.4 %all-gather.18.cloned.1.call-done = bf16[64,84,128]{2,1,0:T(8,128)(2,1)} async-done(((bf16[1,84,128]{2,1,0:T(8,128)(2,1)}), bf16[64,84,128]{2,1,0:T(8,128)(2,1)}) %all-gather.18.cloned.1.call-update) | async-done | bytes 1376272 | tf_op jit(solution)/shard_map/all_gather | solution.py:127
  291.6 3.2 reshape.428
  294.9 135.7 %all-gather.16.cloned.1.call-done = bf16[64,84,128]{2,1,0:T(8,128)(2,1)} async-done(((bf16[1,84,128]{2,1,0:T(8,128)(2,1)}), bf16[64,84,128]{2,1,0:T(8,128)(2,1)}) %all-gather.16.cloned.1.call-update) | async-done | bytes 1376272 | tf_op jit(solution)/shard_map/all_gather | solution.py:128
  430.6 3.2 reshape.426
  433.8 139.1 %all-gather.20.cloned.1.call-done = bf16[64,84,256]{2,1,0:T(8,128)(2,1)} async-done(((bf16[1,84,256]{2,1,0:T(8,128)(2,1)}), bf16[64,84,256]{2,1,0:T(8,128)(2,1)}) %all-gather.20.cloned.1.call-update) | async-done | bytes 2752528 | tf_op jit(solution)/shard_map/all_gather | solution.py:126
  572.9 5.2 reshape.430
  578.1 1.1 constant_dynamic-update-slice_fusion.15
  580.2 1.0 constant_dynamic-update-slice_fusion.13
  582.3 1.1 constant_dynamic-update-slice_fusion.7
  585.7 1.7 multiply_reduce_fusion.3
  587.9 5.1 collective-permute-start.12
  592.9 5.2 collective-permute-start.13
  598.1 2.5 collective-permute-start.14
  600.6 1.5 collective-permute-start.15
  602.1 1.5 collective-permute-start.16
  603.6 1.8 multiply_reduce_fusion.1
  605.8 4.1 convolution_convert_fusion
  610.0 7.4 collective-permute-start.7
  618.2 2.7 collective-permute-start.8
  621.8 3.1 collective-permute-start.9
  624.9 3.3 collective-permute-start.10
  628.2 1.3 collective-permute-start.11
  629.6 2.2 collective-permute-done.10
  631.8 1.4 collective-permute-done.11
  634.4 1.3 fusion.18
  635.8 80.1 %all-gather.14.cloned.1.call-done = bf16[2048,672]{1,0:T(8,128)(2,1)} async-done(((bf16[32,672]{1,0:T(8,128)(2,1)}), bf16[2048,672]{1,0:T(8,128)(2,1)}) %all-gather.14.cloned.1.call-update) | async-done | bytes 2752528 | tf_op jit(solution)/shard_map/all_gather | solution.py:168
  715.9 36.3 %all-gather.12.cloned.1.call-done = bf16[256,2048]{0,1:T(8,128)(2,1)} async-done(((bf16[256,256]{0,1:T(8,128)(2,1)}), bf16[256,2048]{0,1:T(8,128)(2,1)}) %all-gather.12.cloned.1.call-update) | async-done | bytes 1048592 | tf_op jit(solution)/shard_map/all_gather | solution.py:165
  752.1 3.5 multiply_reduce_fusion
  755.7 12.0 %psum.7 = f32[256]{0:T(256)S(1)} all-reduce(f32[256]{0:T(256)S(1)} %get-tuple-element.21), channel_id=1, replica_groups=mesh['seq'=64,'head'=8] {'head'}, use_global_device_ids=true, to_apply=%region_11.12 | all-reduce | flops 256 | bytes 2048 | tf_op jit(solution)/shard_map/psum | solution.py:171
  (114 shorter events, 12.6 us)
Async XLA Ops:
  6.5 6.0 copy-start
  6.5 5.9 copy-start.10
  6.5 9.3 %copy-start.11 = (s32[8]{0:T(128)S(1)}, s32[8]{0:T(128)}, u32[]{:S(2)}) copy-start(s32[8]{0:T(128)} %param.16) | copy-start | bytes 100
  6.5 9.3 %copy-start.15 = (s32[8]{0:T(128)S(1)}, s32[8]{0:T(128)}, u32[]{:S(2)}) copy-start(s32[8]{0:T(128)} %param.17) | copy-start | bytes 100
  6.5 152.3 %copy-start.9 = (bf16[256,672]{0,1:T(8,128)(2,1)S(1)}, bf16[256,672]{0,1:T(8,128)(2,1)}, u32[]{:S(2)}) copy-start(bf16[256,672]{0,1:T(8,128)(2,1)} %param.14) | copy-start | bytes 1032196
  6.5 148.5 %all-gather.10.cloned.1.call-start = ((), (), s32[]{:S(2)}) async-start(), calls=%async_computation | async-start | bytes 3194880 | tf_op jit(solution)/shard_map/all_gather | solution.py:105
  13.7 277.9 %all-gather.18.cloned.1.call-start = ((), (), s32[]{:S(2)}) async-start(), calls=%async_computation.4 | async-start | bytes 1464320 | tf_op jit(solution)/shard_map/all_gather | solution.py:127
  14.5 416.1 %all-gather.16.cloned.1.call-start = ((), (), s32[]{:S(2)}) async-start(), calls=%async_computation.3 | async-start | bytes 1464320 | tf_op jit(solution)/shard_map/all_gather | solution.py:128
  15.2 557.7 %all-gather.20.cloned.1.call-start = ((), (), s32[]{:S(2)}) async-start(), calls=%async_computation.5 | async-start | bytes 2928640 | tf_op jit(solution)/shard_map/all_gather | solution.py:126
  15.8 700.1 %all-gather.14.cloned.1.call-start = ((), (), s32[]{:S(2)}) async-start(), calls=%async_computation.2 | async-start | bytes 3194880 | tf_op jit(solution)/shard_map/all_gather | solution.py:168
  158.9 14.1 %collective-permute-start = (bf16[256,672]{0,1:T(8,128)(2,1)S(1)}, bf16[256,672]{0,1:T(8,128)(2,1)S(1)}, u32[]{:S(2)}, u32[]{:S(2)}) collective-permute-start(bf16[256,672]{0,1:T(8,128)(2,1)S(1)} %select_select_fusion), channel_id=1, source_target_pairs={{0,1},{1,2},{2,3},{3,4},{4,5},{5,6},{6,7},{7,0},{8,9},{9,10},{10,1... | collective-permute-start | bytes 1032200 | tf_op jit(solution)/shard_map/ppermute | solution.py:117
  173.0 6.7 collective-permute-start.1
  179.7 6.7 collective-permute-start.2
  186.4 6.7 collective-permute-start.3
  188.9 563.3 %all-gather.12.cloned.1.call-start = ((), (), s32[]{:S(2)}) async-start(), calls=%async_computation.1 | async-start | bytes 1179648 | tf_op jit(solution)/shard_map/all_gather | solution.py:165
  193.1 7.4 copy-start.4
  193.1 7.4 collective-permute-start.4
  200.4 1.8 copy-start.6
  200.5 8.0 %collective-permute-start.5 = (bf16[256,672]{0,1:T(8,128)(2,1)S(1)}, bf16[256,672]{0,1:T(8,128)(2,1)}, u32[]{:S(2)}, u32[]{:S(2)}) collective-permute-start(bf16[256,672]{0,1:T(8,128)(2,1)S(1)} %collective-permute-done.4), channel_id=1, source_target_pairs={{0,1},{1,2},{2,3},{3,4},{4,5},{5,6},{6,7},{7,0},{8,9},{9,10},{10,1... | collective-permute-start | bytes 1032200 | tf_op jit(solution)/shard_map/ppermute | solution.py:117
  208.5 369.6 %collective-permute-start.6 = (bf16[256,672]{0,1:T(8,128)(2,1)}, bf16[256,672]{0,1:T(8,128)(2,1)}, u32[]{:S(2)}, u32[]{:S(2)}) collective-permute-start(bf16[256,672]{0,1:T(8,128)(2,1)} %collective-permute-done.5), channel_id=1, source_target_pairs={{0,1},{1,2},{2,3},{3,4},{4,5},{5,6},{6,7},{7,0},{8,9},{9,10},{10,1... | collective-permute-start | bytes 1032200 | tf_op jit(solution)/shard_map/ppermute | solution.py:117
  578.1 6.3 copy-start.7
  578.1 6.4 copy-start.5
  582.2 3.5 copy-start.3
  582.2 3.5 copy-start.16
  584.6 2.9 copy-start.13
  584.6 19.0 %copy-start.1 = (bf16[5376,256]{1,0:T(8,128)(2,1)S(1)}, bf16[5376,256]{1,0:T(8,128)(2,1)}, u32[]{:S(2)}) copy-start(bf16[5376,256]{1,0:T(8,128)(2,1)} %reshape.430) | copy-start | bytes 8257540
  584.6 20.8 %copy-start.2 = (bf16[256,10752]{0,1:T(8,128)(2,1)}, bf16[256,10752]{0,1:T(8,128)(2,1)S(1)}, u32[]{:S(2)}) copy-start(bf16[256,10752]{0,1:T(8,128)(2,1)S(1)} %constant_dynamic-update-slice_fusion) | copy-start | bytes 16515076
  587.4 18.2 %copy-start.14 = (f32[128]{0:T(128)S(1)}, f32[128]{0:T(128)}, u32[]{:S(2)}) copy-start(f32[128]{0:T(128)} %param.24) | copy-start | bytes 1540
  587.9 22.2 %collective-permute-start.12 = (bf16[256,128]{0,1:T(8,128)(2,1)S(1)}, bf16[256,128]{0,1:T(8,128)(2,1)}, u32[]{:S(2)}, u32[]{:S(2)}) collective-permute-start(bf16[256,128]{0,1:T(8,128)(2,1)S(1)} %pad_maximum_fusion), channel_id=1, source_target_pairs={{0,32},{8,40},{16,48},{24,56},{32,64},{40,72},{48,80},{56,88},{64,... | collective-permute-start | bytes 196616 | tf_op jit(solution)/shard_map/ppermute | solution.py:20
  592.9 25.3 %collective-permute-start.13 = (bf16[256,128]{0,1:T(8,128)(2,1)S(1)}, bf16[256,128]{0,1:T(8,128)(2,1)}, u32[]{:S(2)}, u32[]{:S(2)}) collective-permute-start(bf16[256,128]{0,1:T(8,128)(2,1)S(1)} %pad_maximum_fusion), channel_id=1, source_target_pairs={{0,24},{8,32},{16,40},{24,48},{32,56},{40,64},{48,72},{56,80},{64,... | collective-permute-start | bytes 196616 | tf_op jit(solution)/shard_map/ppermute | solution.py:20
  598.1 23.7 %collective-permute-start.14 = (bf16[256,128]{0,1:T(8,128)(2,1)S(1)}, bf16[256,128]{0,1:T(8,128)(2,1)S(1)}, u32[]{:S(2)}, u32[]{:S(2)}) collective-permute-start(bf16[256,128]{0,1:T(8,128)(2,1)S(1)} %pad_maximum_fusion), channel_id=1, source_target_pairs={{0,16},{8,24},{16,32},{24,40},{32,48},{40,56},{48,64},{56,72},{64,... | collective-permute-start | bytes 196616 | tf_op jit(solution)/shard_map/ppermute | solution.py:20
  600.6 24.3 %collective-permute-start.15 = (bf16[256,128]{0,1:T(8,128)(2,1)S(1)}, bf16[256,128]{0,1:T(8,128)(2,1)S(1)}, u32[]{:S(2)}, u32[]{:S(2)}) collective-permute-start(bf16[256,128]{0,1:T(8,128)(2,1)S(1)} %pad_maximum_fusion), channel_id=1, source_target_pairs={{0,8},{8,16},{16,24},{24,32},{32,40},{40,48},{48,56},{56,64},{64,7... | collective-permute-start | bytes 196616 | tf_op jit(solution)/shard_map/ppermute | solution.py:20
  602.1 29.7 %collective-permute-start.16 = (bf16[256,128]{0,1:T(8,128)(2,1)S(1)}, bf16[256,128]{0,1:T(8,128)(2,1)S(1)}, u32[]{:S(2)}, u32[]{:S(2)}) collective-permute-start(bf16[256,128]{0,1:T(8,128)(2,1)S(1)} %pad_maximum_fusion), channel_id=1, source_target_pairs={{8,0},{16,8},{24,16},{32,24},{40,32},{48,40},{56,48},{64,56},{72,6... | collective-permute-start | bytes 196616 | tf_op jit(solution)/shard_map/ppermute | solution.py:20
  605.4 4.4 copy-start.8
  610.0 18.2 %collective-permute-start.7 = (bf16[256,128]{1,0:T(8,128)(2,1)S(1)}, bf16[256,128]{1,0:T(8,128)(2,1)S(1)}, u32[]{:S(2)}, u32[]{:S(2)}) collective-permute-start(bf16[256,128]{1,0:T(8,128)(2,1)S(1)} %convolution_convert_fusion), channel_id=1, source_target_pairs={{0,32},{8,40},{16,48},{24,56},{32,64},{40,72},{48,80},{56,88},{64,... | collective-permute-start | bytes 196616 | tf_op jit(solution)/shard_map/ppermute | solution.py:20
  618.2 11.3 %collective-permute-start.8 = (bf16[256,128]{1,0:T(8,128)(2,1)S(1)}, bf16[256,128]{1,0:T(8,128)(2,1)S(1)}, u32[]{:S(2)}, u32[]{:S(2)}) collective-permute-start(bf16[256,128]{1,0:T(8,128)(2,1)S(1)} %convolution_convert_fusion), channel_id=1, source_target_pairs={{0,24},{8,32},{16,40},{24,48},{32,56},{40,64},{48,72},{56,80},{64,... | collective-permute-start | bytes 196616 | tf_op jit(solution)/shard_map/ppermute | solution.py:20
  621.8 7.8 %collective-permute-start.9 = (bf16[256,128]{1,0:T(8,128)(2,1)S(1)}, bf16[256,128]{1,0:T(8,128)(2,1)S(1)}, u32[]{:S(2)}, u32[]{:S(2)}) collective-permute-start(bf16[256,128]{1,0:T(8,128)(2,1)S(1)} %convolution_convert_fusion), channel_id=1, source_target_pairs={{0,16},{8,24},{16,32},{24,40},{32,48},{40,56},{48,64},{56,72},{64,... | collective-permute-start | bytes 196616 | tf_op jit(solution)/shard_map/ppermute | solution.py:20
  624.9 6.8 collective-permute-start.10
  628.2 5.0 collective-permute-start.11
  634.0 133.8 %copy-start.12 = (f32[672]{0:T(1024)S(1)}, f32[672]{0:T(1024)}, u32[]{:S(2)}) copy-start(f32[672]{0:T(1024)} %param.27) | copy-start | bytes 8068
Sparse Core Ops, SparseCore 0:
  13.9 141.1 all-gather.9
  158.0 133.6 all-gather.17
  294.6 135.9 all-gather.15
  433.4 139.4 all-gather.19
  575.7 140.1 all-gather.13
  717.9 34.2 all-gather.11
